TPU v7x, 32 devices: a whole 2x2x4 slice. The times are simulated.
32 devices in a mesh: group: 2 (over x), expert: 16 (over z, y, core).
Axes of the slice: x: 2, y: 2, z: 4, core: 2. Of those that a mesh axis runs over, the one named last changes fastest.
Arguments:
- tokens: bfloat16 [4096, 2048], P(('group', 'expert')), may hold values from -6 to 6
- cotangent: bfloat16 [4096, 2048], P(('group', 'expert')), may hold values from -6 to 6
- gate_probs: float32 [4096, 8], P(('group', 'expert')), may hold values from 0.02 to 0.5
- expert_ids: int32 [4096, 8], P(('group', 'expert')), may hold values from 0 to 15, all different within a row; in each aligned block of 128 rows (0 to 127, 128 to 255, ...) at most 128 rows name the same one
- gate_up: bfloat16 [16, 2048, 768], P('expert'), may hold values from -0.125 to 0.125
- down_weight: bfloat16 [16, 384, 2048], P('expert'), may hold values from -0.3125 to 0.3125
- gate_up_moment: float32 [16, 2048, 768], P('expert', 'group'), may hold values from -6 to 6
- gate_up_second: float32 [16, 2048, 768], P('expert', 'group'), may hold values from 0.05 to 20
- down_moment: float32 [16, 384, 2048], P('expert', None, 'group'), may hold values from -6 to 6
- down_second: float32 [16, 384, 2048], P('expert', None, 'group'), may hold values from 0.05 to 20
Outputs:
- token_grad: bfloat16 [4096, 2048], P(('group', 'expert'))
- updated_gate_up: bfloat16 [16, 2048, 768], P('expert')
- updated_down: bfloat16 [16, 384, 2048], P('expert')
- gate_up_moment_out: float32 [16, 2048, 768], P('expert', 'group')
- gate_up_second_out: float32 [16, 2048, 768], P('expert', 'group')
- down_moment_out: float32 [16, 384, 2048], P('expert', None, 'group')
- down_second_out: float32 [16, 384, 2048], P('expert', None, 'group')
Inputs may be any that keep to these rules, and one draw needn't show every extreme that they name: `expert_ids`: each row names 8 different experts. In the rows of one device no expert is named by more than 128 rows, and in every draw some expert is named by exactly 128 rows of some device.
All inputs are finite; a program needn't handle non-finite values.
Results may differ from a plain program's by a relative error of at most 0.015.
Values may be sent and summed in bfloat16 or wider, within the bound.
A program may use at most 192 MiB of HBM per device.

v0:
```python
import jax
import jax.numpy as jnp
from jax import lax
from jax.sharding import PartitionSpec as P

learn_rate = 0.001
beta_first = 0.9
beta_second = 0.999
adam_eps = 1e-08


def expert_backward(inputs, scaled_grad, weight_gate_up, weight_down):
    hidden_count = weight_down.shape[0]
    projected = jnp.dot(inputs, weight_gate_up, preferred_element_type=jnp.float32)
    gate_part = projected[:, :hidden_count]
    up_part = projected[:, hidden_count:]
    sigmoid_gate = jax.nn.sigmoid(gate_part)
    activated = gate_part * sigmoid_gate
    hidden_act = (activated * up_part).astype(jnp.bfloat16)
    hidden_grad = jnp.dot(scaled_grad, weight_down.T, preferred_element_type=jnp.float32)
    slope = sigmoid_gate * (1.0 + gate_part * (1.0 - sigmoid_gate))
    pair_grad = jnp.concatenate(
        [hidden_grad * up_part * slope, hidden_grad * activated], axis=1
    ).astype(jnp.bfloat16)
    down_grad = jnp.dot(hidden_act.T, scaled_grad, preferred_element_type=jnp.float32)
    gate_up_grad = jnp.dot(inputs.T, pair_grad, preferred_element_type=jnp.float32)
    input_grad = jnp.dot(pair_grad, weight_gate_up.T, preferred_element_type=jnp.float32).astype(
        jnp.bfloat16
    )
    return (gate_up_grad, down_grad, input_grad)


def adam_update(weight, grad, first, second):
    first_new = beta_first * first + (1.0 - beta_first) * grad
    second_new = beta_second * second + (1.0 - beta_second) * grad * grad
    updated = (
        weight.astype(jnp.float32) - learn_rate * first_new / (jnp.sqrt(second_new) + adam_eps)
    ).astype(jnp.bfloat16)
    return (updated, first_new, second_new)


def slot_layout(expert_ids, expert_count, capacity):
    flat_ids = expert_ids.reshape(-1)
    onehot = (flat_ids[:, None] == jnp.arange(expert_count, dtype=jnp.int32)[None, :]).astype(
        jnp.int32
    )
    before = jnp.cumsum(onehot, axis=0) - onehot
    slot_rank = jnp.sum(before * onehot, axis=1)
    return flat_ids * capacity + slot_rank


def local(
    tokens,
    cotangent,
    gate_probs,
    expert_ids,
    gate_up,
    down_weight,
    gate_up_moment,
    gate_up_second,
    down_moment,
    down_second,
):
    expert_count = lax.axis_size("expert")
    local_tokens, model_width = tokens.shape
    top_count = expert_ids.shape[1]
    capacity = min(local_tokens, 9 * local_tokens * top_count // (4 * expert_count))
    slot_total = expert_count * capacity
    slot_index = slot_layout(expert_ids, expert_count, capacity)
    scaled = (gate_probs[:, :, None] * cotangent.astype(jnp.float32)[:, None, :]).astype(
        jnp.bfloat16
    )
    repeated = jnp.broadcast_to(tokens[:, None, :], (local_tokens, top_count, model_width))
    payload = jnp.stack([repeated, scaled], axis=2).reshape(
        local_tokens * top_count, 2, model_width
    )
    outgoing = jnp.zeros((slot_total, 2, model_width), jnp.bfloat16).at[slot_index].set(payload)
    outgoing = outgoing.reshape(expert_count, capacity, 2, model_width)
    received = lax.all_to_all(outgoing, "expert", split_axis=0, concat_axis=0, tiled=True)
    slot_rows = received.reshape(slot_total, 2, model_width)
    weight_pair = gate_up[0]
    weight_down = down_weight[0]
    grad_pair, grad_down, row_grads = expert_backward(
        slot_rows[:, 0], slot_rows[:, 1], weight_pair, weight_down
    )
    returned = lax.all_to_all(
        row_grads.reshape(expert_count, capacity, model_width),
        "expert",
        split_axis=0,
        concat_axis=0,
        tiled=True,
    )
    returned = returned.reshape(slot_total, model_width)
    token_grad = jnp.sum(
        returned[slot_index].reshape(local_tokens, top_count, model_width).astype(jnp.float32),
        axis=1,
    ).astype(jnp.bfloat16)
    sum_pair, sum_down = (
        lax.psum_scatter(
            grad_pair[None].astype(jnp.bfloat16), "group", scatter_dimension=1, tiled=True
        ).astype(jnp.float32),
        lax.psum_scatter(
            grad_down[None].astype(jnp.bfloat16), "group", scatter_dimension=2, tiled=True
        ).astype(jnp.float32),
    )
    group_index = lax.axis_index("group")
    share_rows = model_width // lax.axis_size("group")
    own_pair = lax.dynamic_slice_in_dim(gate_up, group_index * share_rows, share_rows, 1)
    own_down = lax.dynamic_slice_in_dim(down_weight, group_index * share_rows, share_rows, 2)
    new_pair, first_pair, second_pair = adam_update(
        own_pair, sum_pair, gate_up_moment, gate_up_second
    )
    new_down, first_down, second_down = adam_update(own_down, sum_down, down_moment, down_second)
    full_pair, full_down = (
        lax.all_gather(new_pair, "group", axis=1, tiled=True),
        lax.all_gather(new_down, "group", axis=2, tiled=True),
    )
    return (token_grad, full_pair, full_down, first_pair, second_pair, first_down, second_down)


def solution(mesh):
    placed = (
        P(("group", "expert"), None),
        P(("group", "expert"), None),
        P(("group", "expert"), None),
        P(("group", "expert"), None),
        P("expert", None, None),
        P("expert", None, None),
        P("expert", "group", None),
        P("expert", "group", None),
        P("expert", None, "group"),
        P("expert", None, "group"),
    )
    return jax.shard_map(
        local,
        mesh=mesh,
        in_specs=placed,
        out_specs=(
            P(("group", "expert"), None),
            P("expert", None, None),
            P("expert", None, None),
            P("expert", "group", None),
            P("expert", "group", None),
            P("expert", None, "group"),
            P("expert", None, "group"),
        ),
        check_vma=False,
    )
```

profile of v0, /device:TPU:13, one launch (start us, length us, event | category | flops | bytes accessed | tf_op | source)
XLA Modules:
  0.0 805.3 jit_solution(6416571038409245637)
XLA Ops:
  9.1 4.5 reduce-window.6
  16.8 2.4 fusion
  19.2 6.2 pad_maximum_fusion
  25.4 16.4 %copy.31 = bf16[1024,2,2048]{2,1,0:T(2,128)(2,1)} copy(bf16[1024,2,2048]{2,0,1:T(8,128)(2,1)} %pad_maximum_fusion) | data formatting | bytes 16777216 | tf_op jit(solution)/shard_map/stack | solution.py:74
  41.8 10.1 %broadcast_in_dim.2 = bf16[2048,2,2048]{2,1,0:T(2,128)(2,1)} broadcast(bf16[]{:T(256)} %constant.13.clone.1), dimensions={} | broadcast | bytes 16777218 | tf_op jit(solution)/shard_map/broadcast_in_dim | solution.py:77
  51.9 128.3 %scatter_fusion = bf16[2048,2,2048]{2,1,0:T(2,128)(2,1)} fusion(bf16[2048,2,2048]{2,1,0:T(2,128)(2,1)} %broadcast_in_dim.2, s32[1024]{0:T(1024)S(1)} %bitcast.72, bf16[1024,2,2048]{2,1,0:T(2,128)(2,1)} %copy.31), kind=kCustom, calls=%fused_computation.1 | custom fusion | bytes 25169920 | tf_op jit(solution)/shard_map/scatter | solution.py:77
  180.2 368.5 %all_to_all.10 = bf16[16,128,2,2048]{3,2,1,0:T(2,128)(2,1)S(1)} all-to-all(bf16[16,128,2,2048]{3,2,1,0:T(2,128)(2,1)} %bitcast.65), channel_id=1, replica_groups=mesh['group'=2,'expert'=16] {'expert'}, dimensions={0} | all-to-all | bytes 33554432 | tf_op jit(solution)/shard_map/all_to_all | solution.py:79
  548.8 13.5 %copy.32 = bf16[16,128,2,2048]{3,1,0,2:T(8,128)(2,1)S(1)} copy(bf16[16,128,2,2048]{3,2,1,0:T(2,128)(2,1)S(1)} %all_to_all.10) | data formatting | bytes 33554432 | tf_op jit(solution)/shard_map/all_to_all | solution.py:79
  562.3 9.0 %fusion.4 = f32[2048,768]{0,1:T(8,128)} fusion(bf16[2048,2,2048]{2,0,1:T(8,128)(2,1)S(1)} %bitcast.66, bf16[1,2048,768]{2,1,0:T(8,128)(2,1)S(1)} %copy-done.6), kind=kOutput, calls=%fused_computation.11 | convolution fusion | flops 6442450944 | bytes 17825792 | tf_op jit(solution)/shard_map/dot_general | solution.py:14
  571.3 6.5 multiply_convert_fusion.2
  577.8 9.1 %convolution_convert_fusion = bf16[2048,2048]{1,0:T(8,128)(2,1)} fusion(bf16[1,2048,768]{2,1,0:T(8,128)(2,1)S(1)} %copy-done.6, bf16[2048,384]{0,1:T(8,128)(2,1)S(1)} %get-tuple-element.14, bf16[2048,384]{0,1:T(8,128)(2,1)S(1)} %get-tuple-element.13), kind=kOutput, calls=%fused_computation.7 | convolution fusion | flops 6452936704 | bytes 14680064 | tf_op jit(solution)/shard_map/dot_general | solution.py:27
  586.9 6.5 all-to-all-start.1
  593.6 9.9 %fusion.13 = bf16[1,384,2048]{2,1,0:T(8,128)(2,1)} fusion(bf16[2048,2,2048]{2,0,1:T(8,128)(2,1)} %bitcast.68, f32[2048,768]{0,1:T(8,128)} %fusion.4), kind=kOutput, calls=%fused_computation.29 | convolution fusion | flops 3226730496 | bytes 16252928 | tf_op jit(solution)/shard_map/dot_general | solution.py:25
  603.6 10.9 %fusion.11 = bf16[1,2048,768]{2,1,0:T(8,128)(2,1)} fusion(bf16[2048,2,2048]{2,0,1:T(8,128)(2,1)} %bitcast.69, bf16[2048,384]{0,1:T(8,128)(2,1)} %copy-done.8, bf16[2048,384]{0,1:T(8,128)(2,1)S(1)} %get-tuple-element.13), kind=kOutput, calls=%fused_computation.27 | convolution fusion | flops 6450315264 | bytes 14680064 | tf_op jit(solution)/shard_map/dot_general | solution.py:26
  614.6 15.7 %reduce-scatter.5.cloned.1.call-done = bf16[1,384,1024]{2,1,0:T(8,128)(2,1)} async-done(((bf16[1,384,2048]{2,1,0:T(8,128)(2,1)}), bf16[1,384,1024]{2,1,0:T(8,128)(2,1)}) %reduce-scatter.5.cloned.1.call-update) | async-done | bytes 786448 | tf_op jit(solution)/shard_map/reduce_scatter | solution.py:102
  630.3 4.6 subtract_convert_fusion.1
  635.2 41.4 %reduce-scatter.3.cloned.1.call-done = bf16[1,1024,768]{2,1,0:T(8,128)(2,1)} async-done(((bf16[1,2048,768]{2,1,0:T(8,128)(2,1)}), bf16[1,1024,768]{2,1,0:T(8,128)(2,1)}) %reduce-scatter.3.cloned.1.call-update) | async-done | bytes 1572880 | tf_op jit(solution)/shard_map/reduce_scatter | solution.py:99
  676.5 8.2 %subtract_convert_fusion = (bf16[1,1024,768]{2,1,0:T(8,128)(2,1)}, f32[1,1024,768]{2,1,0:T(8,128)}, f32[1,1024,768]{2,1,0:T(8,128)}) fusion(bf16[1,2048,768]{2,1,0:T(8,128)(2,1)} %param.14, s32[]{:T(128)S(6)} %select_n.16, bf16[1,1024,768]{2,1,0:T(8,128)(2,1)} %reduce-scatter.3.cloned.1.call-done, f32[1,1024,768]{2,1,0:T(8,128)} %param.16, ...), kind=kLoop, calls=%fused_computation.22 | loop fusion | flops 11010048 | bytes 17301508 | tf_op jit(solution)/shard_map/convert_element_type | solution.py:38
  684.8 20.5 %all-gather.5.cloned.1.call-done = bf16[1,384,2048]{2,1,0:T(8,128)(2,1)} async-done(((bf16[1,384,1024]{2,1,0:T(8,128)(2,1)}), bf16[1,384,2048]{2,1,0:T(8,128)(2,1)}) %all-gather.5.cloned.1.call-update) | async-done | bytes 1572880 | tf_op jit(solution)/shard_map/all_gather | solution.py:116
  705.3 46.9 %all-gather.3.cloned.1.call-done = bf16[1,2048,768]{2,1,0:T(8,128)(2,1)} async-done(((bf16[1,1024,768]{2,1,0:T(8,128)(2,1)}), bf16[1,2048,768]{2,1,0:T(8,128)(2,1)}) %all-gather.3.cloned.1.call-update) | async-done | bytes 3145744 | tf_op jit(solution)/shard_map/all_gather | solution.py:115
  752.3 23.4 %all-to-all-done.1 = bf16[16,128,2048]{2,1,0:T(8,128)(2,1)} async-done(((bf16[16,128,2048]{2,1,0:T(8,128)(2,1)}), bf16[16,128,2048]{2,1,0:T(8,128)(2,1)}, u32[]{:S(2)}, u32[]{:S(2)}) %all-to-all-start.1) | async-done | bytes 8388640 | tf_op jit(solution)/shard_map/all_to_all | solution.py:86
  775.7 13.3 %gather_fusion = bf16[1024,2048]{1,0:T(8,128)(2,1)} fusion(bf16[2048,2048]{1,0:T(8,128)(2,1)} %bitcast.13, s32[1024]{0:T(1024)S(1)} %broadcast_clamp_fusion), kind=kCustom, calls=%fused_computation | custom fusion | bytes 8392704 | tf_op jit(solution)/shard_map/gather | solution.py:95
  789.0 6.0 bitcast_reduce_fusion
  795.0 1.7 copy.38
  (47 shorter events, 7.8 us)
Async XLA Ops:
  7.2 8.9 %copy-start = (bf16[128,2048]{1,0:T(8,128)(2,1)S(1)}, bf16[128,2048]{1,0:T(8,128)(2,1)}, u32[]{:S(2)}) copy-start(bf16[128,2048]{1,0:T(8,128)(2,1)} %param.10) | copy-start | bytes 1572868
  548.8 13.5 %copy-start.6 = (bf16[1,2048,768]{2,1,0:T(8,128)(2,1)S(1)}, bf16[1,2048,768]{2,1,0:T(8,128)(2,1)}, u32[]{:S(2)}) copy-start(bf16[1,2048,768]{2,1,0:T(8,128)(2,1)} %param.14) | copy-start | bytes 9437188
  562.3 9.1 %copy-start.2 = (bf16[16,128,2,2048]{3,1,0,2:T(8,128)(2,1)}, bf16[16,128,2,2048]{3,1,0,2:T(8,128)(2,1)S(1)}, u32[]{:S(2)}) copy-start(bf16[16,128,2,2048]{3,1,0,2:T(8,128)(2,1)S(1)} %copy.32) | copy-start | bytes 50331652
  562.3 9.1 %copy-start.7 = (bf16[1,384,2048]{2,1,0:T(8,128)(2,1)S(1)}, bf16[1,384,2048]{2,1,0:T(8,128)(2,1)}, u32[]{:S(2)}) copy-start(bf16[1,384,2048]{2,1,0:T(8,128)(2,1)} %param.15) | copy-start | bytes 4718596
  577.8 9.1 %copy-start.8 = (bf16[2048,384]{0,1:T(8,128)(2,1)}, bf16[2048,384]{0,1:T(8,128)(2,1)S(1)}, u32[]{:S(2)}) copy-start(bf16[2048,384]{0,1:T(8,128)(2,1)S(1)} %get-tuple-element.14) | copy-start | bytes 4718596
  586.9 188.8 %all-to-all-start.1 = ((bf16[16,128,2048]{2,1,0:T(8,128)(2,1)}), bf16[16,128,2048]{2,1,0:T(8,128)(2,1)}, u32[]{:S(2)}, u32[]{:S(2)}) async-start(bf16[16,128,2048]{2,1,0:T(8,128)(2,1)} %bitcast.70), calls=%async_computation.1 | async-start | bytes 16777216 | tf_op jit(solution)/shard_map/all_to_all | solution.py:86
  593.4 36.9 %reduce-scatter.5.cloned.1.call-start = ((), (), s32[]{:S(2)}) async-start(), calls=%async_computation.6 | async-start | bytes 2359296 | tf_op jit(solution)/shard_map/reduce_scatter | solution.py:102
  603.5 73.0 %reduce-scatter.3.cloned.1.call-start = ((), (), s32[]{:S(2)}) async-start(), calls=%async_computation.4 | async-start | bytes 4718592 | tf_op jit(solution)/shard_map/reduce_scatter | solution.py:99
  614.5 15.8 %copy-start.5 = (f32[1,384,1024]{2,1,0:T(8,128)S(1)}, f32[1,384,1024]{2,1,0:T(8,128)}, u32[]{:S(2)}) copy-start(f32[1,384,1024]{2,1,0:T(8,128)} %param.18) | copy-start | bytes 4718596
  614.5 90.8 %all-gather.5.cloned.1.call-start = ((), (), s32[]{:S(2)}) async-start(), calls=%async_computation.7 | async-start | bytes 2359296 | tf_op jit(solution)/shard_map/all_gather | solution.py:116
  634.9 117.4 %all-gather.3.cloned.1.call-start = ((), (), s32[]{:S(2)}) async-start(), calls=%async_computation.5 | async-start | bytes 4718592 | tf_op jit(solution)/shard_map/all_gather | solution.py:115
  789.0 6.0 copy-start.3
  795.0 2.5 copy-start.4
  795.0 3.7 copy-start.1
Sparse Core Ops, SparseCore 0:
  603.7 26.5 reduce-scatter.4
  633.2 43.3 reduce-scatter.2
  678.1 27.1 all-gather.4
  707.3 44.9 all-gather.2
where the time goes:
time: 807 us; the launch traced here: 805 us
  blocking collectives  369 us (46%)
  local copies, waits for them, and re-layouts  188 us (23%)
  waiting for transfers between devices  148 us (18%)
  matrix products  45.3 us (6%)
  other arithmetic  34 us (4%)
  between operations  13.9 us (2%)
    all_to_all x1, blocking collectives, local(): lax.all_to_all(outgoing, 'expert', split_axis=0, concat_axis=0, tiled=True)  369 us
    scatter x1, local copies, waits for them, and re-layouts, local(): jnp.zeros((slot_total, 2, model_width), jnp.bfloat16).at[slot_index]  128 us
    all_gather x1, waiting for transfers between devices, local(): lax.all_gather(new_pair, 'group', axis=1, tiled=True)  46.9 us
    reduce_scatter x1, waiting for transfers between devices, local(): lax.psum_scatter(grad_pair[None].astype(jnp.bfloat16), 'group', scatter_d...  41.4 us
    all_to_all x1, waiting for transfers between devices, local(): lax.all_to_all(row_grads.reshape(expert_count, capacity, model_width), 'e...  23.4 us
    all_gather x1, waiting for transfers between devices, local(): lax.all_gather(new_down, 'group', axis=2, tiled=True)  20.5 us
    another operation x2, local copies, waits for them, and re-layouts, local(): jnp.stack([repeated, scaled], axis=2)  17.1 us
  transfers between devices with their start and end apart: 5, of which 5 were waited for; matrix products, arithmetic and copies ran while one was open for 4% of the time, Pallas kernels for 0%

commit v1 on v0

v1 whole, which is shorter than its diff:
```python
import jax
import jax.numpy as jnp
from jax import lax
from jax.sharding import PartitionSpec as P

learn_rate = 0.001
beta_first = 0.9
beta_second = 0.999
adam_eps = 1e-08


def adam_update(weight, grad, first, second):
    first_new = beta_first * first + (1.0 - beta_first) * grad
    second_new = beta_second * second + (1.0 - beta_second) * grad * grad
    updated = (
        weight.astype(jnp.float32) - learn_rate * first_new / (jnp.sqrt(second_new) + adam_eps)
    ).astype(jnp.bfloat16)
    return (updated, first_new, second_new)


def contract(a, b, dims):
    return lax.dot_general(a, b, (dims, ((), ())), preferred_element_type=jnp.float32)


def local(
    tokens,
    cotangent,
    gate_probs,
    expert_ids,
    gate_up,
    down_weight,
    gate_up_moment,
    gate_up_second,
    down_moment,
    down_second,
):
    expert_count = lax.axis_size("expert")
    model_width = tokens.shape[1]
    me = lax.axis_index("expert")
    experts = jnp.arange(expert_count, dtype=jnp.int32)
    dense = jnp.sum(
        jnp.where(expert_ids[:, :, None] == experts, gate_probs[:, :, None], 0.0), axis=1
    )
    weights = lax.all_gather(dense, "expert", axis=0, tiled=True)
    weight = lax.dynamic_slice_in_dim(weights, me, 1, 1)
    all_tokens = lax.all_gather(tokens, "expert", axis=0, tiled=True)
    all_cotangent = lax.all_gather(cotangent, "expert", axis=0, tiled=True)
    weight_pair = gate_up[0]
    weight_down = down_weight[0]
    hidden_count = weight_down.shape[0]
    projected = contract(all_tokens, weight_pair, ((1,), (0,)))
    gate_part = projected[:, :hidden_count]
    up_part = projected[:, hidden_count:]
    sigmoid_gate = jax.nn.sigmoid(gate_part)
    activated = gate_part * sigmoid_gate
    hidden_act = (weight * activated * up_part).astype(jnp.bfloat16)
    hidden_grad = weight * contract(all_cotangent, weight_down, ((1,), (1,)))
    slope = sigmoid_gate * (1.0 + gate_part * (1.0 - sigmoid_gate))
    pair_grad = jnp.concatenate(
        [hidden_grad * up_part * slope, hidden_grad * activated], axis=1
    ).astype(jnp.bfloat16)
    grad_pair = contract(all_tokens, pair_grad, ((0,), (0,))).astype(jnp.bfloat16)
    sum_pair = lax.psum_scatter(grad_pair[None], "group", scatter_dimension=1, tiled=True)
    row_grads = contract(pair_grad, weight_pair, ((1,), (1,))).astype(jnp.bfloat16)
    token_grad = lax.psum_scatter(row_grads, "expert", scatter_dimension=0, tiled=True)
    grad_down = contract(hidden_act, all_cotangent, ((0,), (0,))).astype(jnp.bfloat16)
    sum_down = lax.psum_scatter(grad_down[None], "group", scatter_dimension=2, tiled=True)
    group_index = lax.axis_index("group")
    share_rows = model_width // lax.axis_size("group")
    own_pair = lax.dynamic_slice_in_dim(gate_up, group_index * share_rows, share_rows, 1)
    own_down = lax.dynamic_slice_in_dim(down_weight, group_index * share_rows, share_rows, 2)
    new_pair, first_pair, second_pair = adam_update(
        own_pair, sum_pair.astype(jnp.float32), gate_up_moment, gate_up_second
    )
    new_down, first_down, second_down = adam_update(
        own_down, sum_down.astype(jnp.float32), down_moment, down_second
    )
    full_pair = lax.all_gather(new_pair, "group", axis=1, tiled=True)
    full_down = lax.all_gather(new_down, "group", axis=2, tiled=True)
    return (token_grad, full_pair, full_down, first_pair, second_pair, first_down, second_down)


def solution(mesh):
    placed = (
        P(("group", "expert"), None),
        P(("group", "expert"), None),
        P(("group", "expert"), None),
        P(("group", "expert"), None),
        P("expert", None, None),
        P("expert", None, None),
        P("expert", "group", None),
        P("expert", "group", None),
        P("expert", None, "group"),
        P("expert", None, "group"),
    )
    return jax.shard_map(
        local,
        mesh=mesh,
        in_specs=placed,
        out_specs=(
            P(("group", "expert"), None),
            P("expert", None, None),
            P("expert", None, None),
            P("expert", "group", None),
            P("expert", "group", None),
            P("expert", None, "group"),
            P("expert", None, "group"),
        ),
        check_vma=False,
    )
```

time: 807 us -> 438 us (0.54)
  blocking collectives: 369 us -> 16.1 us
  waiting for transfers between devices: 148 us -> 311 us
  local copies, waits for them, and re-layouts: 188 us -> 27.7 us
  other arithmetic: 34 us -> 14.4 us
    all_to_all x1 -> x0, blocking collectives: 369 us -> none  [local(): lax.all_to_all(outgoing, 'expert', split_axis=0, concat_axis=0, tiled=True)]
    scatter x1 -> x0, local copies, waits for them, and re-layouts: 128 us -> none  [local(): jnp.zeros((slot_total, 2, model_width), jnp.bfloat16).at[slot_index]]
    all_gather x2 -> x4, waiting for transfers between devices: 67.5 us -> 172 us  [the longest x1 64.5 us: local(): all_cotangent = lax.all_gather(cotangent, 'expert', axis=0, tiled=True)]
    reduce_scatter x2 -> x3, waiting for transfers between devices: 57.1 us -> 138 us  [the longest x1 105 us: local(): lax.psum_scatter(row_grads, 'expert', scatter_dimension=0, tiled=True)]
    all_to_all x1 -> x0, waiting for transfers between devices: 23.4 us -> none  [local(): lax.all_to_all(row_grads.reshape(expert_count, capacity, model_width), 'e...]
    unnamed x22 -> x13, local copies, waits for them, and re-layouts: 5.3 us -> 26.4 us
    another operation x4 -> x0, local copies, waits for them, and re-layouts: 17.2 us -> none  [the longest x2 17.1 us: local(): jnp.stack([repeated, scaled], axis=2)]
    all_gather x0 -> x1, blocking collectives: none -> 16.1 us  [local(): weights = lax.all_gather(dense, 'expert', axis=0, tiled=True)]
  transfers between devices with their start and end apart: 5 -> 7, of which waited for: 5 -> 7; matrix products, arithmetic and copies ran while one was open for 4% -> 18% of each run, Pallas kernels for 0% -> 0%
where the time goes in v1:
time: 438 us; the launch traced here: 436 us
  waiting for transfers between devices  311 us (71%)
  matrix products  52.1 us (12%)
  local copies, waits for them, and re-layouts  27.7 us (6%)
  blocking collectives  16.1 us (4%)
  other arithmetic  14.4 us (3%)
  between operations  14.2 us (3%)
    reduce_scatter x1, waiting for transfers between devices, local(): lax.psum_scatter(row_grads, 'expert', scatter_dimension=0, tiled=True)  105 us
    all_gather x1, waiting for transfers between devices, local(): all_cotangent = lax.all_gather(cotangent, 'expert', axis=0, tiled=True)  64.5 us
    all_gather x1, waiting for transfers between devices, local(): all_tokens = lax.all_gather(tokens, 'expert', axis=0, tiled=True)  59.7 us
    dot_general x5, matrix products, contract(): lax.dot_general(a, b, (dims, ((), ())), preferred_element_type=jnp.float32)  52.1 us
    all_gather x1, waiting for transfers between devices, local(): full_pair = lax.all_gather(new_pair, 'group', axis=1, tiled=True)  39.3 us
    reduce_scatter x1, waiting for transfers between devices, local(): lax.psum_scatter(grad_pair[None], 'group', scatter_dimension=1, tiled=True)  29.4 us
    unnamed x13, local copies, waits for them, and re-layouts  26.4 us
    all_gather x1, blocking collectives, local(): weights = lax.all_gather(dense, 'expert', axis=0, tiled=True)  16.1 us
  transfers between devices with their start and end apart: 7, of which 7 were waited for; matrix products, arithmetic and copies ran while one was open for 18% of the time, Pallas kernels for 0%

profile of v1, /device:TPU:13, one launch (start us, length us, event | category | flops | bytes accessed | tf_op | source)
XLA Modules:
  0.0 436.3 jit_solution(3301466971305791338)
XLA Ops:
  9.4 16.1 %all_gather.15 = f32[2048,16]{0,1:T(8,128)S(1)} all-gather(f32[128,16]{0,1:T(8,128)S(1)} %select_reduce_fusion), channel_id=1, replica_groups=mesh['group'=2,'expert'=16] {'expert'}, dimensions={0}, use_global_device_ids=true | all-gather | bytes 139264 | tf_op jit(solution)/shard_map/all_gather | solution.py:44
  25.6 59.7 %all-gather.7.cloned.1.call-done = bf16[2048,2048]{1,0:T(8,128)(2,1)} async-done(((bf16[128,2048]{1,0:T(8,128)(2,1)}), bf16[2048,2048]{1,0:T(8,128)(2,1)}) %all-gather.7.cloned.1.call-update) | async-done | bytes 8388624 | tf_op jit(solution)/shard_map/all_gather | solution.py:46
  85.3 10.8 %fusion.3 = f32[2048,768]{0,1:T(8,128)} fusion(bf16[2048,2048]{1,0:T(8,128)(2,1)} %all-gather.7.cloned.1.call-done, bf16[1,2048,768]{2,1,0:T(8,128)(2,1)S(1)} %copy-done), kind=kOutput, calls=%fused_computation.8 | convolution fusion | flops 6442450944 | bytes 17825792 | tf_op jit(solution)/shard_map/dot_general | solution.py:22
  96.1 64.5 %all-gather.5.cloned.1.call-done = bf16[2048,2048]{1,0:T(8,128)(2,1)} async-done(((bf16[128,2048]{1,0:T(8,128)(2,1)}), bf16[2048,2048]{1,0:T(8,128)(2,1)}) %all-gather.5.cloned.1.call-update) | async-done | bytes 8388624 | tf_op jit(solution)/shard_map/all_gather | solution.py:47
  160.6 9.9 %fusion.7 = bf16[1,384,2048]{2,1,0:T(8,128)(2,1)} fusion(bf16[2048,2048]{1,0:T(8,128)(2,1)} %all-gather.5.cloned.1.call-done, f32[2048,768]{0,1:T(8,128)} %fusion.3, f32[2048]{0:T(1024)S(1)} %bitcast.21), kind=kOutput, calls=%fused_computation.19 | convolution fusion | flops 3227516928 | bytes 16261120 | tf_op jit(solution)/shard_map/dot_general | solution.py:22
  170.8 9.9 %multiply_convert_fusion.2 = (bf16[2048,384]{0,1:T(8,128)(2,1)S(1)}, bf16[2048,384]{0,1:T(8,128)(2,1)S(1)}) fusion(f32[2048,768]{0,1:T(8,128)} %fusion.3, bf16[2048,2048]{1,0:T(8,128)(2,1)} %all-gather.5.cloned.1.call-done, bf16[1,384,2048]{2,1,0:T(8,128)(2,1)} %param.15, f32[2048]{0:T(1024)S(1)} %bitcast.22), kind=kOutput, calls=%fused_computation.13 | convolution fusion | flops 3232235520 | bytes 19406848 | tf_op jit(solution)/shard_map/dot_general | solution.py:22
  180.7 1.1 copy-done.1
  182.4 10.3 %fusion.6 = bf16[1,2048,768]{1,2,0:T(8,128)(2,1)} fusion(bf16[2048,2048]{1,0:T(8,128)(2,1)} %all-gather.7.cloned.1.call-done, bf16[2048,384]{0,1:T(8,128)(2,1)S(1)} %get-tuple-element.35, bf16[2048,384]{0,1:T(8,128)(2,1)S(1)} %get-tuple-element.34), kind=kOutput, calls=%fused_computation.17 | convolution fusion | flops 6450315264 | bytes 14680064 | tf_op jit(solution)/shard_map/dot_general | solution.py:22
  192.7 3.4 reduce-scatter.8.cloned.1.call-done
  196.2 5.1 %subtract_convert_fusion.1 = (bf16[1,384,1024]{2,1,0:T(8,128)(2,1)}, f32[1,384,1024]{2,1,0:T(8,128)}, f32[1,384,1024]{2,1,0:T(8,128)}) fusion(bf16[1,384,2048]{2,1,0:T(8,128)(2,1)} %param.15, s32[]{:T(128)S(6)} %select_n.13, bf16[1,384,1024]{2,1,0:T(8,128)(2,1)} %reduce-scatter.8.cloned.1.call-done, f32[1,384,1024]{2,1,0:T(8,128)} %param.18, ...), kind=kLoop, calls=%fused_computation.25 | loop fusion | flops 5505024 | bytes 8650756 | tf_op jit(solution)/shard_map/convert_element_type | solution.py:17
  201.3 1.3 constant_dynamic-slice_fusion
  202.5 2.6 copy.39
  205.1 4.2 copy.34
  209.4 3.5 copy.35
  212.9 29.4 %reduce-scatter.6.cloned.1.call-done = bf16[1,1024,768]{1,2,0:T(8,128)(2,1)} async-done(((bf16[1,2048,768]{1,2,0:T(8,128)(2,1)}), bf16[1,1024,768]{1,2,0:T(8,128)(2,1)}) %reduce-scatter.6.cloned.1.call-update) | async-done | bytes 1572880 | tf_op jit(solution)/shard_map/reduce_scatter | solution.py:63
  242.3 8.6 %subtract_convert_fusion = (bf16[1,1024,768]{1,2,0:T(8,128)(2,1)}, f32[1,1024,768]{1,2,0:T(8,128)}, f32[1,1024,768]{1,2,0:T(8,128)}) fusion(bf16[1,1024,768]{1,2,0:T(8,128)(2,1)} %copy.39, bf16[1,1024,768]{1,2,0:T(8,128)(2,1)} %reduce-scatter.6.cloned.1.call-done, f32[1,1024,768]{1,2,0:T(8,128)} %copy.34, f32[1,1024,768]{1,2,0:T(8,128)} %copy.35), kind=kLoop, calls=%fused_computation.11 | loop fusion | flops 11010048 | bytes 17301504 | tf_op jit(solution)/shard_map/convert_element_type | solution.py:17
  251.2 11.2 %convolution_convert_fusion = bf16[2048,2048]{1,0:T(8,128)(2,1)} fusion(bf16[1,2048,768]{2,1,0:T(8,128)(2,1)S(1)} %copy-done, bf16[2048,384]{0,1:T(8,128)(2,1)} %copy-done.2, bf16[2048,384]{0,1:T(8,128)(2,1)} %copy-done.1), kind=kOutput, calls=%fused_computation | convolution fusion | flops 6452936704 | bytes 14680064 | tf_op jit(solution)/shard_map/dot_general | solution.py:22
  262.4 8.6 %all-gather.11.cloned.1.call-done = bf16[1,384,2048]{2,1,0:T(8,128)(2,1)} async-done(((bf16[1,384,1024]{2,1,0:T(8,128)(2,1)}), bf16[1,384,2048]{2,1,0:T(8,128)(2,1)}) %all-gather.11.cloned.1.call-update) | async-done | bytes 1572880 | tf_op jit(solution)/shard_map/all_gather | solution.py:79
  270.9 3.5 copy.37
  274.5 3.5 copy.38
  278.0 39.3 %all-gather.9.cloned.1.call-done = bf16[1,2048,768]{1,2,0:T(8,128)(2,1)} async-done(((bf16[1,1024,768]{1,2,0:T(8,128)(2,1)}), bf16[1,2048,768]{1,2,0:T(8,128)(2,1)}) %all-gather.9.cloned.1.call-update) | async-done | bytes 3145744 | tf_op jit(solution)/shard_map/all_gather | solution.py:78
  317.3 4.6 %copy.36 = bf16[1,2048,768]{2,1,0:T(8,128)(2,1)} copy(bf16[1,2048,768]{1,2,0:T(8,128)(2,1)} %all-gather.9.cloned.1.call-done) | data formatting | bytes 6291456
  321.9 104.8 %reduce-scatter.4.cloned.1.call-done = bf16[128,2048]{1,0:T(8,128)(2,1)} async-done(((bf16[2048,2048]{1,0:T(8,128)(2,1)}), bf16[128,2048]{1,0:T(8,128)(2,1)}) %reduce-scatter.4.cloned.1.call-update) | async-done | bytes 524304 | tf_op jit(solution)/shard_map/reduce_scatter | solution.py:65
  426.7 2.7 copy.41
  (21 shorter events, 3.4 us)
Async XLA Ops:
  7.2 78.1 %copy-start = (bf16[1,2048,768]{2,1,0:T(8,128)(2,1)S(1)}, bf16[1,2048,768]{2,1,0:T(8,128)(2,1)}, u32[]{:S(2)}) copy-start(bf16[1,2048,768]{2,1,0:T(8,128)(2,1)} %param.14) | copy-start | bytes 9437188
  7.2 78.1 %all-gather.7.cloned.1.call-start = ((), (), s32[]{:S(2)}) async-start(), calls=%async_computation.4 | async-start | bytes 8912896 | tf_op jit(solution)/shard_map/all_gather | solution.py:46
  7.9 152.7 %all-gather.5.cloned.1.call-start = ((), (), s32[]{:S(2)}) async-start(), calls=%async_computation.3 | async-start | bytes 8912896 | tf_op jit(solution)/shard_map/all_gather | solution.py:47
  8.7 187.5 %reduce-scatter.8.cloned.1.call-start = ((), (), s32[]{:S(2)}) async-start(), calls=%async_computation.8 | async-start | bytes 2359296 | tf_op jit(solution)/shard_map/reduce_scatter | solution.py:67
  170.6 71.7 %reduce-scatter.6.cloned.1.call-start = ((), (), s32[]{:S(2)}) async-start(), calls=%async_computation.6 | async-start | bytes 4718592 | tf_op jit(solution)/shard_map/reduce_scatter | solution.py:63
  180.7 1.2 copy-start.1
  180.7 1.7 copy-start.2
  192.7 78.2 %all-gather.11.cloned.1.call-start = ((), (), s32[]{:S(2)}) async-start(), calls=%async_computation.9 | async-start | bytes 2359296 | tf_op jit(solution)/shard_map/all_gather | solution.py:79
  201.2 116.1 %all-gather.9.cloned.1.call-start = ((), (), s32[]{:S(2)}) async-start(), calls=%async_computation.7 | async-start | bytes 4718592 | tf_op jit(solution)/shard_map/all_gather | solution.py:78
  250.9 175.8 %reduce-scatter.4.cloned.1.call-start = ((), (), s32[]{:S(2)}) async-start(), calls=%async_computation.5 | async-start | bytes 8912896 | tf_op jit(solution)/shard_map/reduce_scatter | solution.py:65
Sparse Core Ops, SparseCore 0:
  10.2 75.0 all-gather.6
  87.5 73.1 all-gather.4
  170.7 25.4 reduce-scatter.7
  198.9 43.3 reduce-scatter.5
  243.7 27.2 all-gather.10
  272.3 44.9 all-gather.8
  321.9 104.7 reduce-scatter.3

commit v2 on v1

--- a/solution.py
+++ b/solution.py
@@ -22,6 +22,31 @@
     return lax.dot_general(a, b, (dims, ((), ())), preferred_element_type=jnp.float32)
 
 
+def group_reduce(partial, dim):
+    size = lax.axis_size("group")
+    share = partial.shape[dim] // size
+    own = lax.axis_index("group")
+    total = lax.dynamic_slice_in_dim(partial, own * share, share, dim)
+    for step in range(1, size):
+        sent = lax.dynamic_slice_in_dim(partial, (own + step) % size * share, share, dim)
+        pairs = [(i, (i + step) % size) for i in range(size)]
+        total = total + lax.ppermute(sent.astype(jnp.bfloat16), "group", pairs).astype(jnp.float32)
+    return total
+
+
+def group_gather(block, dim):
+    size = lax.axis_size("group")
+    share = block.shape[dim]
+    own = lax.axis_index("group")
+    whole = jnp.zeros(block.shape[:dim] + (share * size,) + block.shape[dim + 1 :], block.dtype)
+    whole = lax.dynamic_update_slice_in_dim(whole, block, own * share, dim)
+    for step in range(1, size):
+        pairs = [(i, (i + step) % size) for i in range(size)]
+        came = lax.ppermute(block, "group", pairs)
+        whole = lax.dynamic_update_slice_in_dim(whole, came, (own - step) % size * share, dim)
+    return whole
+
+
 def local(
     tokens,
     cotangent,
@@ -41,10 +66,21 @@
     dense = jnp.sum(
         jnp.where(expert_ids[:, :, None] == experts, gate_probs[:, :, None], 0.0), axis=1
     )
-    weights = lax.all_gather(dense, "expert", axis=0, tiled=True)
-    weight = lax.dynamic_slice_in_dim(weights, me, 1, 1)
+    high = dense.astype(jnp.bfloat16)
+    low = (dense - high.astype(jnp.float32)).astype(jnp.bfloat16)
+    pad = -2 * expert_count % 128
+    side = jnp.concatenate([high, low, jnp.zeros((tokens.shape[0], pad), jnp.bfloat16)], axis=1)
     all_tokens = lax.all_gather(tokens, "expert", axis=0, tiled=True)
-    all_cotangent = lax.all_gather(cotangent, "expert", axis=0, tiled=True)
+    gathered = lax.all_gather(
+        jnp.concatenate([cotangent, side], axis=1), "expert", axis=0, tiled=True
+    )
+    all_cotangent = gathered[:, :model_width]
+    weight = sum(
+        lax.dynamic_slice_in_dim(gathered, model_width + part * expert_count + me, 1, 1).astype(
+            jnp.float32
+        )
+        for part in range(2)
+    )
     weight_pair = gate_up[0]
     weight_down = down_weight[0]
     hidden_count = weight_down.shape[0]
@@ -59,24 +95,25 @@
     pair_grad = jnp.concatenate(
         [hidden_grad * up_part * slope, hidden_grad * activated], axis=1
     ).astype(jnp.bfloat16)
-    grad_pair = contract(all_tokens, pair_grad, ((0,), (0,))).astype(jnp.bfloat16)
-    sum_pair = lax.psum_scatter(grad_pair[None], "group", scatter_dimension=1, tiled=True)
     row_grads = contract(pair_grad, weight_pair, ((1,), (1,))).astype(jnp.bfloat16)
+    row_grads, pair_grad = lax.optimization_barrier((row_grads, pair_grad))
     token_grad = lax.psum_scatter(row_grads, "expert", scatter_dimension=0, tiled=True)
-    grad_down = contract(hidden_act, all_cotangent, ((0,), (0,))).astype(jnp.bfloat16)
-    sum_down = lax.psum_scatter(grad_down[None], "group", scatter_dimension=2, tiled=True)
+    grad_pair = contract(all_tokens, pair_grad, ((0,), (0,)))
+    sum_pair = group_reduce(grad_pair, 0)[None]
+    grad_down = contract(hidden_act, all_cotangent, ((0,), (0,)))
+    sum_down = group_reduce(grad_down, 1)[None]
     group_index = lax.axis_index("group")
     share_rows = model_width // lax.axis_size("group")
     own_pair = lax.dynamic_slice_in_dim(gate_up, group_index * share_rows, share_rows, 1)
     own_down = lax.dynamic_slice_in_dim(down_weight, group_index * share_rows, share_rows, 2)
     new_pair, first_pair, second_pair = adam_update(
-        own_pair, sum_pair.astype(jnp.float32), gate_up_moment, gate_up_second
+        own_pair, sum_pair, gate_up_moment, gate_up_second
     )
     new_down, first_down, second_down = adam_update(
-        own_down, sum_down.astype(jnp.float32), down_moment, down_second
+        own_down, sum_down, down_moment, down_second
     )
-    full_pair = lax.all_gather(new_pair, "group", axis=1, tiled=True)
-    full_down = lax.all_gather(new_down, "group", axis=2, tiled=True)
+    full_pair = group_gather(new_pair, 1)
+    full_down = group_gather(new_down, 2)
     return (token_grad, full_pair, full_down, first_pair, second_pair, first_down, second_down)
 
 

time: 438 us -> 325 us (0.74)
  waiting for transfers between devices: 311 us -> 198 us
  blocking collectives: 16.1 us -> 0 us
  local copies, waits for them, and re-layouts: 27.7 us -> 38.9 us
    reduce_scatter x1, waiting for transfers between devices: 105 us -> 0.01 us  [local(): lax.psum_scatter(row_grads, 'expert', scatter_dimension=0, tiled=True)]
    ppermute x0 -> x4, waiting for transfers between devices: none -> 55.2 us  [the longest x2 33.6 us: group_gather(): came = lax.ppermute(block, 'group', pairs)]
    all_gather x3 -> x1, waiting for transfers between devices: 112 us -> 68.4 us  [local(): lax.all_gather(jnp.concatenate([cotangent, side], axis=1), 'expert', axis...]
    reduce_scatter x2 -> x0, waiting for transfers between devices: 32.8 us -> none  [the longest x1 29.4 us: local(): lax.psum_scatter(grad_pair[None], 'group', scatter_dimension=1, tiled=True)]
    all_gather x1 -> x0, blocking collectives: 16.1 us -> none  [local(): weights = lax.all_gather(dense, 'expert', axis=0, tiled=True)]
    all_gather x1, waiting for transfers between devices: 59.7 us -> 74.1 us  [local(): all_tokens = lax.all_gather(tokens, 'expert', axis=0, tiled=True)]
    convert_element_type x2 -> x1, other arithmetic: 13.6 us -> 7.37 us  [adam_update(): updated = (weight.astype(jnp.float32) - learn_rate * first_new / (jnp.sqr...]
    convert_element_type x0 -> x5, local copies, waits for them, and re-layouts: none -> 5.21 us  [the longest x1 2.58 us: adam_update(): updated = (weight.astype(jnp.float32) - learn_rate * first_new / (jnp.sqr...]
  transfers between devices with their start and end apart: 7 -> 7, of which waited for: 7 -> 5; matrix products, arithmetic and copies ran while one was open for 18% -> 24% of each run, Pallas kernels for 0% -> 0%
where the time goes in v2:
time: 325 us; the launch traced here: 321 us
  waiting for transfers between devices  198 us (61%)
  matrix products  49.3 us (15%)
  local copies, waits for them, and re-layouts  38.9 us (12%)
  other arithmetic  17.1 us (5%)
  between operations  13.9 us (4%)
  starting transfers between devices  3.72 us (1%)
    all_gather x1, waiting for transfers between devices, local(): all_tokens = lax.all_gather(tokens, 'expert', axis=0, tiled=True)  74.1 us
    all_gather x1, waiting for transfers between devices, local(): lax.all_gather(jnp.concatenate([cotangent, side], axis=1), 'expert', axis...  68.4 us
    dot_general x5, matrix products, contract(): lax.dot_general(a, b, (dims, ((), ())), preferred_element_type=jnp.float32)  49.3 us
    ppermute x2, waiting for transfers between devices, group_gather(): came = lax.ppermute(block, 'group', pairs)  33.6 us
    unnamed x23, local copies, waits for them, and re-layouts  22.7 us
    ppermute x2, waiting for transfers between devices, group_reduce(): lax.ppermute(sent.astype(jnp.bfloat16), 'group', pairs).astype(jnp.float32)  21.6 us
    convert_element_type x1, other arithmetic, adam_update(): updated = (weight.astype(jnp.float32) - learn_rate * first_new / (jnp.sqr...  7.37 us
  transfers between devices with their start and end apart: 7, of which 5 were waited for; matrix products, arithmetic and copies ran while one was open for 24% of the time, Pallas kernels for 0%

profile of v2, /device:TPU:13, one launch (start us, length us, event | category | flops | bytes accessed | tf_op | source)
XLA Modules:
  0.0 321.2 jit_solution(11332989226028586108)
XLA Ops:
  11.0 74.1 %all-gather.5.cloned.1.call-done = bf16[2048,2048]{1,0:T(8,128)(2,1)} async-done(((bf16[128,2048]{1,0:T(8,128)(2,1)}), bf16[2048,2048]{1,0:T(8,128)(2,1)}) %all-gather.5.cloned.1.call-update) | async-done | bytes 8388624 | tf_op jit(solution)/shard_map/all_gather | solution.py:73
  85.1 10.8 %fusion.7 = f32[2048,768]{0,1:T(8,128)} fusion(bf16[2048,2048]{1,0:T(8,128)(2,1)} %all-gather.5.cloned.1.call-done, bf16[1,2048,768]{2,1,0:T(8,128)(2,1)S(1)} %copy-done), kind=kOutput, calls=%fused_computation.12 | convolution fusion | flops 6442450944 | bytes 17825792 | tf_op jit(solution)/shard_map/dot_general | solution.py:22
  95.9 68.4 %all-gather.3.cloned.1.call-done = bf16[2048,2176]{1,0:T(8,128)(2,1)} async-done(((bf16[128,2176]{1,0:T(8,128)(2,1)}), bf16[2048,2176]{1,0:T(8,128)(2,1)}) %all-gather.3.cloned.1.call-update) | async-done | bytes 8912912 | tf_op jit(solution)/shard_map/all_gather | solution.py:74
  164.3 2.0 add_reduce_fusion
  166.3 9.9 %multiply_convert_fusion.2 = (bf16[2048,384]{0,1:T(8,128)(2,1)S(1)}, bf16[2048,384]{0,1:T(8,128)(2,1)S(1)}) fusion(f32[2048,768]{0,1:T(8,128)} %fusion.7, bf16[1,384,2048]{2,1,0:T(8,128)(2,1)} %param.15, bf16[2048,2176]{1,0:T(8,128)(2,1)} %all-gather.3.cloned.1.call-done, f32[2048]{0:T(1024)S(1)} %add_reduce_fusion), kind=kOutput, calls=%fused_computation.18 | convolution fusion | flops 3232235520 | bytes 19406848 | tf_op jit(solution)/shard_map/dot_general | solution.py:22
  176.2 2.1 pad_maximum_fusion
  178.3 9.1 %convolution_convert_fusion = bf16[2048,2048]{1,0:T(8,128)(2,1)} fusion(bf16[1,2048,768]{2,1,0:T(8,128)(2,1)S(1)} %copy-done, bf16[2048,384]{0,1:T(8,128)(2,1)S(1)} %get-tuple-element.42, bf16[2048,384]{0,1:T(8,128)(2,1)S(1)} %get-tuple-element.41), kind=kOutput, calls=%fused_computation | convolution fusion | flops 6452936704 | bytes 14680064 | tf_op jit(solution)/shard_map/dot_general | solution.py:22
  187.4 10.2 %fusion.22 = f32[768,2048]{1,0:T(8,128)S(1)} fusion(bf16[2048,768]{0,1:T(8,128)(2,1)} %pad_maximum_fusion, bf16[2048,2048]{1,0:T(8,128)(2,1)} %all-gather.5.cloned.1.call-done), kind=kOutput, calls=%fused_computation.42 | convolution fusion | flops 6442450944 | bytes 17825792 | tf_op jit(solution)/shard_map/dot_general | solution.py:22
  197.7 2.8 copy-done.5
  204.3 2.7 copy.44
  207.0 3.8 %copy.38 = f32[1,1024,768]{1,2,0:T(8,128)} copy(f32[1,1024,768]{2,1,0:T(8,128)} %param.16) | data formatting | bytes 6291456 | tf_op args[6]
  210.8 3.5 %copy.39 = f32[1,1024,768]{1,2,0:T(8,128)} copy(f32[1,1024,768]{2,1,0:T(8,128)} %param.17) | data formatting | bytes 6291456 | tf_op args[7]
  214.3 9.3 %fusion = f32[384,2048]{1,0:T(8,128)S(1)} fusion(bf16[2048,2176]{1,0:T(8,128)(2,1)} %all-gather.3.cloned.1.call-done, f32[2048,768]{0,1:T(8,128)} %fusion.7, f32[2048]{0:T(1024)S(1)} %add_reduce_fusion), kind=kOutput, calls=%fused_computation.1 | convolution fusion | flops 3226730496 | bytes 17833984 | tf_op jit(solution)/shard_map/dot_general | solution.py:22
  224.6 13.3 %collective-permute-done = bf16[1024,768]{0,1:T(8,128)(2,1)} collective-permute-done((bf16[1024,768]{0,1:T(8,128)(2,1)}, bf16[1024,768]{0,1:T(8,128)(2,1)}, u32[]{:S(2)}, u32[]{:S(2)}) %collective-permute-start) | collective-permute-done | bytes 1572896 | tf_op jit(solution)/shard_map/ppermute | solution.py:33
  237.9 7.4 %subtract_convert_fusion = (bf16[1,1024,768]{1,2,0:T(8,128)(2,1)}, f32[1,1024,768]{1,2,0:T(8,128)}, f32[1,1024,768]{1,2,0:T(8,128)}) fusion(bf16[1,1024,768]{1,2,0:T(8,128)(2,1)S(1)} %copy-done.3, bf16[1024,768]{0,1:T(8,128)(2,1)} %collective-permute-done, f32[768,2048]{1,0:T(8,128)} %copy-done.5, s32[]{:T(128)S(6)} %select_n.44, ...), kind=kLoop, calls=%fused_computation.15 | loop fusion | flops 11796480 | bytes 20447236 | tf_op jit(solution)/shard_map/convert_element_type | solution.py:17
  246.5 8.3 %collective-permute-done.2 = bf16[384,1024]{1,0:T(8,128)(2,1)} collective-permute-done((bf16[384,1024]{1,0:T(8,128)(2,1)}, bf16[384,1024]{1,0:T(8,128)(2,1)}, u32[]{:S(2)}, u32[]{:S(2)}) %collective-permute-start.2) | collective-permute-done | bytes 786464 | tf_op jit(solution)/shard_map/ppermute | solution.py:33
  254.9 4.8 %constant_dynamic-update-slice_fusion.1 = (bf16[1,384,2048]{2,1,0:T(8,128)(2,1)S(1)}, bf16[1,384,1024]{2,1,0:T(8,128)(2,1)}, f32[1,384,1024]{2,1,0:T(8,128)}, f32[1,384,1024]{2,1,0:T(8,128)}) fusion(bf16[1,384,2048]{2,1,0:T(8,128)(2,1)S(1)} %broadcast_in_dim.30, s32[]{:T(128)S(6)} %select_n.44, bf16[1,384,2048]{2,1,0:T(8,128)(2,1)} %param.15, ...), kind=kLoop, calls=%fused_computation.37 | loop fusion | flops 5898240 | bytes 11010052 | tf_op jit(solution)/shard_map/dynamic_update_slice | solution.py:42
  262.0 2.6 copy.40
  264.6 3.5 %copy.42 = f32[1,1024,768]{2,1,0:T(8,128)} copy(f32[1,1024,768]{1,2,0:T(8,128)} %get-tuple-element.37) | data formatting | bytes 6291456
  268.2 3.5 %copy.43 = f32[1,1024,768]{2,1,0:T(8,128)} copy(f32[1,1024,768]{1,2,0:T(8,128)} %get-tuple-element.38) | data formatting | bytes 6291456
  271.7 33.6 %collective-permute-done.3 = bf16[1,384,1024]{2,1,0:T(8,128)(2,1)} collective-permute-done((bf16[1,384,1024]{2,1,0:T(8,128)(2,1)}, bf16[1,384,1024]{2,1,0:T(8,128)(2,1)}, u32[]{:S(2)}, u32[]{:S(2)}) %collective-permute-start.3) | collective-permute-done | bytes 786464 | tf_op jit(solution)/shard_map/ppermute | solution.py:45
  305.3 2.1 constant_dynamic-update-slice_fusion
  309.4 2.6 copy.41
  312.1 2.7 constant_dynamic-update-slice_fusion.2
  (41 shorter events, 14.4 us)
Async XLA Ops:
  7.2 78.0 %copy-start = (bf16[1,2048,768]{2,1,0:T(8,128)(2,1)S(1)}, bf16[1,2048,768]{2,1,0:T(8,128)(2,1)}, u32[]{:S(2)}) copy-start(bf16[1,2048,768]{2,1,0:T(8,128)(2,1)} %param.14) | copy-start | bytes 9437188
  7.2 77.9 %all-gather.5.cloned.1.call-start = ((), (), s32[]{:S(2)}) async-start(), calls=%async_computation.2 | async-start | bytes 8912896 | tf_op jit(solution)/shard_map/all_gather | solution.py:73
  7.9 156.4 %all-gather.3.cloned.1.call-start = ((), (), s32[]{:S(2)}) async-start(), calls=%async_computation.1 | async-start | bytes 9469952 | tf_op jit(solution)/shard_map/all_gather | solution.py:74
  11.0 303.7 %reduce-scatter.2.cloned.1.call-start = ((), (), s32[]{:S(2)}) async-start(), calls=%async_computation.3 | async-start | bytes 8912896 | tf_op jit(solution)/shard_map/reduce_scatter | solution.py:100
  197.7 2.8 copy-start.5
  201.8 36.1 %collective-permute-start = (bf16[1024,768]{0,1:T(8,128)(2,1)}, bf16[1024,768]{0,1:T(8,128)(2,1)}, u32[]{:S(2)}, u32[]{:S(2)}) collective-permute-start(bf16[1024,768]{0,1:T(8,128)(2,1)} %fusion.15), channel_id=1, source_target_pairs={{0,16},{16,0},{1,17},{17,1},{2,18},{18,2},{3,19},{19,3},{4,20},{20... | collective-permute-start | bytes 4718600 | tf_op jit(solution)/shard_map/ppermute | solution.py:33
  214.3 23.6 %copy-start.1 = (f32[1,1024,768]{1,2,0:T(8,128)S(1)}, f32[1,1024,768]{1,2,0:T(8,128)}, u32[]{:S(2)}) copy-start(f32[1,1024,768]{1,2,0:T(8,128)} %copy.38) | copy-start | bytes 9437188
  214.3 23.6 %copy-start.2 = (f32[1,1024,768]{1,2,0:T(8,128)S(1)}, f32[1,1024,768]{1,2,0:T(8,128)}, u32[]{:S(2)}) copy-start(f32[1,1024,768]{1,2,0:T(8,128)} %copy.39) | copy-start | bytes 9437188
  214.3 23.6 %copy-start.3 = (bf16[1,1024,768]{1,2,0:T(8,128)(2,1)S(1)}, bf16[1,1024,768]{1,2,0:T(8,128)(2,1)}, u32[]{:S(2)}) copy-start(bf16[1,1024,768]{1,2,0:T(8,128)(2,1)} %copy.44) | copy-start | bytes 4718596
  224.6 30.3 %copy-start.8 = (f32[1,384,1024]{2,1,0:T(8,128)S(1)}, f32[1,384,1024]{2,1,0:T(8,128)}, u32[]{:S(2)}) copy-start(f32[1,384,1024]{2,1,0:T(8,128)} %param.18) | copy-start | bytes 4718596
  224.6 30.1 %collective-permute-start.2 = (bf16[384,1024]{1,0:T(8,128)(2,1)}, bf16[384,1024]{1,0:T(8,128)(2,1)}, u32[]{:S(2)}, u32[]{:S(2)}) collective-permute-start(bf16[384,1024]{1,0:T(8,128)(2,1)} %dynamic-slice_convert_fusion.1), channel_id=1, source_target_pairs={{0,16},{16,0},{1,17},{17,1},{2,18},{18,2},{3,19},{19,3},{4,20},{20... | collective-permute-start | bytes 2359304 | tf_op jit(solution)/shard_map/ppermute | solution.py:33
  245.3 64.2 %collective-permute-start.1 = (bf16[1,1024,768]{1,2,0:T(8,128)(2,1)}, bf16[1,1024,768]{1,2,0:T(8,128)(2,1)}, u32[]{:S(2)}, u32[]{:S(2)}) collective-permute-start(bf16[1,1024,768]{1,2,0:T(8,128)(2,1)} %get-tuple-element.36), channel_id=1, source_target_pairs={{0,16},{16,0},{1,17},{17,1},{2,18},{18,2},{3,19},{19,3},{4,20},{20... | collective-permute-start | bytes 4718600 | tf_op jit(solution)/shard_map/ppermute | solution.py:45
  259.7 1.1 copy-start.7
  260.8 44.5 %collective-permute-start.3 = (bf16[1,384,1024]{2,1,0:T(8,128)(2,1)}, bf16[1,384,1024]{2,1,0:T(8,128)(2,1)}, u32[]{:S(2)}, u32[]{:S(2)}) collective-permute-start(bf16[1,384,1024]{2,1,0:T(8,128)(2,1)} %get-tuple-element.33), channel_id=1, source_target_pairs={{0,16},{16,0},{1,17},{17,1},{2,18},{18,2},{3,19},{19,3},{4,20},{20... | collective-permute-start | bytes 2359304 | tf_op jit(solution)/shard_map/ppermute | solution.py:45
  271.7 35.9 %copy-start.4 = (bf16[1,1024,768]{2,1,0:T(8,128)(2,1)S(1)}, bf16[1,1024,768]{2,1,0:T(8,128)(2,1)}, u32[]{:S(2)}) copy-start(bf16[1,1024,768]{2,1,0:T(8,128)(2,1)} %copy.40) | copy-start | bytes 4718596
  307.8 1.7 copy-start.6
Sparse Core Ops, SparseCore 0:
  10.2 74.9 all-gather.4
  88.0 76.2 all-gather.2
  187.6 104.0 reduce-scatter.1

commit v3 on v2

--- a/solution.py
+++ b/solution.py
@@ -1,6 +1,10 @@
+import functools
+
 import jax
 import jax.numpy as jnp
 from jax import lax
+from jax.experimental import pallas as pl
+from jax.experimental.pallas import tpu as pltpu
 from jax.sharding import PartitionSpec as P
 
 learn_rate = 0.001
@@ -45,6 +49,127 @@
         came = lax.ppermute(block, "group", pairs)
         whole = lax.dynamic_update_slice_in_dim(whole, came, (own - step) % size * share, dim)
     return whole
+
+
+LINE = 4
+CORES = 2
+
+
+def gather_kernel(size, first_ref, second_ref, first_out, second_out, send_sem, recv_sem, own_sem):
+    rows = size // (LINE * CORES)
+    me = lax.axis_index("expert")
+    core = me % CORES
+    col = me // CORES % rows
+    line = me // (CORES * rows)
+    sources, outs = (first_ref, second_ref), (first_out, second_out)
+
+    def device(at_line, at_col, at_core):
+        return (at_line * rows + at_col) * CORES + at_core
+
+    steps = {
+        "up": (line < LINE - 1, device(line + 1, col, core)),
+        "down": (line > 0, device(line - 1, col, core)),
+        "right": (col < rows - 1, device(line, col + 1, core)),
+        "left": (col > 0, device(line, col - 1, core)),
+        "sibling": (core >= 0, device(line, col, 1 - core)),
+    }
+
+    barrier = pltpu.get_barrier_semaphore()
+    for exists, target in steps.values():
+        @pl.when(exists)
+        def _(target=target):
+            pl.semaphore_signal(
+                barrier, inc=1, device_id={"expert": target}, device_id_type=pl.DeviceIdType.MESH
+            )
+    count = 1
+    for name in ("up", "down", "right", "left"):
+        count = count + jnp.where(steps[name][0], 1, 0)
+    pl.semaphore_wait(barrier, count)
+
+    sends = []
+
+    def copy(kind, block, target, sem, src):
+        return pltpu.make_async_remote_copy(
+            src_ref=src,
+            dst_ref=outs[kind].at[block],
+            send_sem=send_sem.at[sem],
+            recv_sem=recv_sem.at[kind, block],
+            device_id={"expert": target},
+            device_id_type=pl.DeviceIdType.MESH,
+        )
+
+    def forward(kind, block, valid, names, src=None):
+        for name in names:
+            exists, target = steps[name]
+            sem = len(sends)
+            sends.append((valid & exists, kind, block, target, sem, src))
+
+            @pl.when(valid & exists)
+            def _():
+                copy(kind, block, target, sem, outs[kind].at[block] if src is None else src).start()
+
+    def arrive(kind, block, valid):
+        @pl.when(valid)
+        def _():
+            copy(kind, block, steps["sibling"][1], 0, outs[kind].at[block]).wait_recv()
+
+    always = core >= 0
+    for kind in range(2):
+        forward(
+            kind, me, always, ("right", "left", "up", "down", "sibling"), sources[kind]
+        )
+    for kind in range(2):
+        pltpu.make_async_copy(sources[kind], outs[kind].at[me], own_sem.at[kind]).start()
+    lanes = [(line, always)]
+    for far in range(1, LINE):
+        for kind in range(2):
+            for at_line, valid, onward in (
+                (line - far, line >= far, "up"),
+                (line + far, line < LINE - far, "down"),
+            ):
+                block = device(at_line, col, core)
+                arrive(kind, block, valid)
+                forward(kind, block, valid, ("right", "left", onward, "sibling"))
+        lanes += [(line - far, line >= far), (line + far, line < LINE - far)]
+    for far in range(1, rows):
+        for at_line, valid in lanes:
+            for kind in range(2):
+                for at_col, within, onward in (
+                    (col - far, col >= far, "right"),
+                    (col + far, col < rows - far, "left"),
+                ):
+                    block = device(at_line, at_col, core)
+                    arrive(kind, block, valid & within)
+                    forward(kind, block, valid & within, (onward, "sibling"))
+    for at_line in range(LINE):
+        for at_col in range(rows):
+            for kind in range(2):
+                arrive(kind, device(at_line, at_col, 1 - core), always)
+    for kind in range(2):
+        pltpu.make_async_copy(sources[kind], outs[kind].at[me], own_sem.at[kind]).wait()
+    for valid, kind, block, target, sem, src in sends:
+        @pl.when(valid)
+        def _():
+            copy(kind, block, target, sem, outs[kind].at[block] if src is None else src).wait_send()
+
+
+def gather_pair(first, second):
+    size = lax.axis_size("expert")
+    rows = size // (LINE * CORES)
+    send_count = 2 * (5 + 8 * (LINE - 1) + 4 * (rows - 1) * (2 * LINE - 1))
+    outs = pl.pallas_call(
+        functools.partial(gather_kernel, size),
+        out_shape=[jax.ShapeDtypeStruct((size,) + x.shape, x.dtype) for x in (first, second)],
+        in_specs=[pl.BlockSpec(memory_space=pl.ANY)] * 2,
+        out_specs=[pl.BlockSpec(memory_space=pl.ANY)] * 2,
+        scratch_shapes=[
+            pltpu.SemaphoreType.DMA((send_count,)),
+            pltpu.SemaphoreType.DMA((2, size)),
+            pltpu.SemaphoreType.DMA((2,)),
+        ],
+        compiler_params=pltpu.CompilerParams(collective_id=0, has_side_effects=True),
+    )(first, second)
+    return [x.reshape(-1, x.shape[-1]) for x in outs]
 
 
 def local(
@@ -70,10 +195,7 @@
     low = (dense - high.astype(jnp.float32)).astype(jnp.bfloat16)
     pad = -2 * expert_count % 128
     side = jnp.concatenate([high, low, jnp.zeros((tokens.shape[0], pad), jnp.bfloat16)], axis=1)
-    all_tokens = lax.all_gather(tokens, "expert", axis=0, tiled=True)
-    gathered = lax.all_gather(
-        jnp.concatenate([cotangent, side], axis=1), "expert", axis=0, tiled=True
-    )
+    all_tokens, gathered = gather_pair(tokens, jnp.concatenate([cotangent, side], axis=1))
     all_cotangent = gathered[:, :model_width]
     weight = sum(
         lax.dynamic_slice_in_dim(gathered, model_width + part * expert_count + me, 1, 1).astype(

time: 325 us -> 268 us (0.82)
  waiting for transfers between devices: 198 us -> 75.7 us
  Pallas kernels: 0 us -> 99.5 us
  local copies, waits for them, and re-layouts: 38.9 us -> 16 us
  matrix products: 49.3 us -> 43.9 us
  other arithmetic: 17.1 us -> 11.8 us
    all_gather x2 -> x0, waiting for transfers between devices: 142 us -> none  [the longest x1 74.1 us: local(): all_tokens = lax.all_gather(tokens, 'expert', axis=0, tiled=True)]
    pallas_call x0 -> x1, Pallas kernels: none -> 99.5 us  [gather_pair(): pl.pallas_call(functools.partial(gather_kernel, size), out_shape=[jax.Sha...]
    unnamed x23 -> x32, local copies, waits for them, and re-layouts: 22.7 us -> 6.89 us
    ppermute x2, waiting for transfers between devices: 33.6 us -> 45.1 us  [group_gather(): came = lax.ppermute(block, 'group', pairs)]
    ppermute x2, waiting for transfers between devices: 21.6 us -> 30.5 us  [group_reduce(): lax.ppermute(sent.astype(jnp.bfloat16), 'group', pairs).astype(jnp.float32)]
    convert_element_type x1, other arithmetic: 7.37 us -> 0.01 us  [local(): high = dense.astype(jnp.bfloat16)]
    dynamic_update_slice x1 -> x2, other arithmetic: 4.75 us -> 10.9 us  [group_gather(): whole = lax.dynamic_update_slice_in_dim(whole, block, own * share, dim)]
    dot_general x5, matrix products: 49.3 us -> 43.9 us  [contract(): lax.dot_general(a, b, (dims, ((), ())), preferred_element_type=jnp.float32)]
  transfers between devices with their start and end apart: 7 -> 5, of which waited for: 5 -> 3; matrix products, arithmetic and copies ran while one was open for 24% -> 13% of each run, Pallas kernels for 0% -> 0%
where the time goes in v3:
time: 268 us; the launch traced here: 265 us
  Pallas kernels  99.5 us (37%)
  waiting for transfers between devices  75.7 us (28%)
  matrix products  43.9 us (16%)
  local copies, waits for them, and re-layouts  16 us (6%)
  between operations  14.4 us (5%)
  other arithmetic  11.8 us (4%)
  starting transfers between devices  3.98 us (1%)
    pallas_call x1, Pallas kernels, gather_pair(): pl.pallas_call(functools.partial(gather_kernel, size), out_shape=[jax.Sha...  99.5 us
    ppermute x2, waiting for transfers between devices, group_gather(): came = lax.ppermute(block, 'group', pairs)  45.1 us
    dot_general x5, matrix products, contract(): lax.dot_general(a, b, (dims, ((), ())), preferred_element_type=jnp.float32)  43.9 us
    ppermute x2, waiting for transfers between devices, group_reduce(): lax.ppermute(sent.astype(jnp.bfloat16), 'group', pairs).astype(jnp.float32)  30.5 us
    dynamic_update_slice x2, other arithmetic, group_gather(): whole = lax.dynamic_update_slice_in_dim(whole, block, own * share, dim)  10.9 us
    unnamed x32, local copies, waits for them, and re-layouts  6.89 us
  transfers between devices with their start and end apart: 5, of which 3 were waited for; matrix products, arithmetic and copies ran while one was open for 13% of the time, Pallas kernels for 0%

profile of v3, /device:TPU:13, one launch (start us, length us, event | category | flops | bytes accessed | tf_op | source)
XLA Modules:
  0.0 265.3 jit_solution(15552393322460452895)
XLA Ops:
  7.2 0.7 select_reduce_fusion
  8.3 1.9 concatenate.7.second_ref
  10.2 99.5 %shard_map.153 = (bf16[16,128,2048]{2,1,0:T(8,128)(2,1)}, bf16[16,128,2176]{2,1,0:T(8,128)(2,1)}) custom-call(bf16[128,2048]{1,0:T(8,128)(2,1)} %first_ref.1, bf16[128,2176]{1,0:T(8,128)(2,1)} %concatenate.7.second_ref), custom_call_target="tpu_custom_call" | custom-call | tf_op jit(solution)/shard_map/pallas_call | solution.py:160
  109.7 1.7 constant_dynamic-slice_fusion.1
  111.9 10.5 %fusion.7 = f32[2048,768]{0,1:T(8,128)S(1)} fusion(bf16[2048,2048]{1,0:T(8,128)(2,1)} %bitcast.39, bf16[1,2048,768]{2,1,0:T(8,128)(2,1)} %param.14), kind=kOutput, calls=%fused_computation.11 | convolution fusion | flops 6442450944 | bytes 17825792 | tf_op jit(solution)/shard_map/dot_general | solution.py:26
  122.5 4.6 %multiply_convert_fusion.2 = (bf16[2048,384]{0,1:T(8,128)(2,1)S(1)}, bf16[2048,384]{0,1:T(8,128)(2,1)S(1)}) fusion(f32[2048,768]{0,1:T(8,128)S(1)} %fusion.7, bf16[1,384,2048]{2,1,0:T(8,128)(2,1)S(1)} %copy-done.9, bf16[2048,2176]{1,0:T(8,128)(2,1)S(1)} %bitcast.36, f32[2048]{0:T(1024)S(1)} %bitcast.37), kind=kOutput, calls=%fused_computation.18 | convolution fusion | flops 3232235520 | bytes 19406848 | tf_op jit(solution)/shard_map/dot_general | solution.py:26
  127.4 1.7 copy-done.8
  129.1 9.1 %convolution_convert_fusion = bf16[2048,2048]{1,0:T(8,128)(2,1)} fusion(bf16[1,2048,768]{2,1,0:T(8,128)(2,1)S(1)} %copy-done.8, bf16[2048,384]{0,1:T(8,128)(2,1)S(1)} %get-tuple-element.24, bf16[2048,384]{0,1:T(8,128)(2,1)S(1)} %get-tuple-element.23), kind=kOutput, calls=%fused_computation | convolution fusion | flops 6452936704 | bytes 14680064 | tf_op jit(solution)/shard_map/dot_general | solution.py:26
  138.2 9.4 %fusion.21 = f32[2048,768]{1,0:T(8,128)S(1)} fusion(bf16[2048,2048]{1,0:T(8,128)(2,1)} %bitcast.40, bf16[2048,768]{0,1:T(8,128)(2,1)S(1)} %pad_maximum_fusion), kind=kOutput, calls=%fused_computation.42 | convolution fusion | flops 6442450944 | bytes 17825792 | tf_op jit(solution)/shard_map/dot_general | solution.py:26
  147.6 2.8 %copy-done = f32[2048,768]{1,0:T(8,128)} copy-done((f32[2048,768]{1,0:T(8,128)}, f32[2048,768]{1,0:T(8,128)S(1)}, u32[]{:S(2)}) %copy-start) | copy-done | bytes 6291480
  150.4 1.3 dynamic-slice_convert_fusion
  151.7 1.2 collective-permute-start
  153.0 10.2 %fusion = f32[384,2048]{1,0:T(8,128)S(1)} fusion(bf16[2048,2176]{1,0:T(8,128)(2,1)} %bitcast.33, f32[2048,768]{0,1:T(8,128)} %copy-done.11, f32[2048]{0:T(1024)S(1)} %bitcast.38), kind=kOutput, calls=%fused_computation.1 | convolution fusion | flops 3226730496 | bytes 17833984 | tf_op jit(solution)/shard_map/dot_general | solution.py:26
  163.2 1.6 copy-done.3
  164.8 1.0 dynamic-slice_convert_fusion.1
  166.0 22.1 %collective-permute-done = bf16[1024,768]{1,0:T(8,128)(2,1)} collective-permute-done((bf16[1024,768]{1,0:T(8,128)(2,1)}, bf16[1024,768]{1,0:T(8,128)(2,1)}, u32[]{:S(2)}, u32[]{:S(2)}) %collective-permute-start) | collective-permute-done | bytes 1572896 | tf_op jit(solution)/shard_map/ppermute | solution.py:37
  188.4 6.9 %constant_dynamic-update-slice_fusion.3 = (bf16[1,2048,768]{2,1,0:T(8,128)(2,1)S(1)}, bf16[1,1024,768]{2,1,0:T(8,128)(2,1)}, f32[1,1024,768]{2,1,0:T(8,128)}, f32[1,1024,768]{2,1,0:T(8,128)}) fusion(bf16[1,2048,768]{2,1,0:T(8,128)(2,1)S(1)} %broadcast_in_dim.29, s32[]{:T(128)S(6)} %select_n.44, bf16[1,2048,768]{2,1,0:T(8,128)(2,1)} %param.14, ...), kind=kLoop, calls=%fused_computation.38 | loop fusion | flops 11796480 | bytes 22020100 | tf_op jit(solution)/shard_map/dynamic_update_slice | solution.py:46
  195.3 1.2 collective-permute-start.1
  196.6 8.4 %collective-permute-done.2 = bf16[384,1024]{1,0:T(8,128)(2,1)} collective-permute-done((bf16[384,1024]{1,0:T(8,128)(2,1)}, bf16[384,1024]{1,0:T(8,128)(2,1)}, u32[]{:S(2)}, u32[]{:S(2)}) %collective-permute-start.2) | collective-permute-done | bytes 786464 | tf_op jit(solution)/shard_map/ppermute | solution.py:37
  205.2 3.9 %constant_dynamic-update-slice_fusion.1 = (bf16[1,384,2048]{2,1,0:T(8,128)(2,1)S(1)}, bf16[1,384,1024]{2,1,0:T(8,128)(2,1)}, f32[1,384,1024]{2,1,0:T(8,128)}, f32[1,384,1024]{2,1,0:T(8,128)}) fusion(bf16[1,384,2048]{2,1,0:T(8,128)(2,1)S(1)} %broadcast_in_dim.30, s32[]{:T(128)S(6)} %select_n.44, bf16[1,384,2048]{2,1,0:T(8,128)(2,1)S(1)} %copy-done.10, ...), kind=kLoop, calls=%fused_computation.36 | loop fusion | flops 5898240 | bytes 11010052 | tf_op jit(solution)/shard_map/dynamic_update_slice | solution.py:46
  209.2 1.3 collective-permute-start.3
  210.4 45.1 %collective-permute-done.3 = bf16[1,384,1024]{2,1,0:T(8,128)(2,1)} collective-permute-done((bf16[1,384,1024]{2,1,0:T(8,128)(2,1)}, bf16[1,384,1024]{2,1,0:T(8,128)(2,1)}, u32[]{:S(2)}, u32[]{:S(2)}) %collective-permute-start.3) | collective-permute-done | bytes 786464 | tf_op jit(solution)/shard_map/ppermute | solution.py:49
  255.6 1.2 constant_dynamic-update-slice_fusion
  256.8 1.3 constant_dynamic-update-slice_fusion.2
  (45 shorter events, 2.1 us)
Async XLA Ops:
  7.2 251.0 %reduce-scatter.2.cloned.1.call-start = ((), (), s32[]{:S(2)}) async-start(), calls=%async_computation.1 | async-start | bytes 8912896 | tf_op jit(solution)/shard_map/reduce_scatter | solution.py:222
  111.4 11.1 %slice-start = ((s8[8912896]{0:T(1024)(128)(4,1)}), s8[524288]{0:T(1024)(128)(4,1)S(1)}, s32[]{:S(2)}) async-start(s8[8912896]{0:T(1024)(128)(4,1)} %bitcast.34), calls=%async_computation.2 | async-start | bytes 1048576
  111.9 10.6 %copy-start.9 = (bf16[1,384,2048]{2,1,0:T(8,128)(2,1)S(1)}, bf16[1,384,2048]{2,1,0:T(8,128)(2,1)}, u32[]{:S(2)}) copy-start(bf16[1,384,2048]{2,1,0:T(8,128)(2,1)} %param.15) | copy-start | bytes 4718596
  111.9 10.6 %slice-start.1 = ((s8[8912896]{0:T(1024)(128)(4,1)}), s8[4194304]{0:T(1024)(128)(4,1)S(1)}, s32[]{:S(2)}) async-start(s8[8912896]{0:T(1024)(128)(4,1)} %bitcast.34), calls=%async_computation.3 | async-start | bytes 8388608
  111.9 10.6 %slice-start.2 = ((s8[8912896]{0:T(1024)(128)(4,1)}), s8[4194304]{0:T(1024)(128)(4,1)S(1)}, s32[]{:S(2)}) async-start(s8[8912896]{0:T(1024)(128)(4,1)} %bitcast.34), calls=%async_computation.4 | async-start | bytes 8388608
  122.5 4.7 %copy-start.11 = (f32[2048,768]{0,1:T(8,128)}, f32[2048,768]{0,1:T(8,128)S(1)}, u32[]{:S(2)}) copy-start(f32[2048,768]{0,1:T(8,128)S(1)} %fusion.7) | copy-start | bytes 18874372
  127.2 1.9 copy-start.8
  147.6 2.8 %copy-start = (f32[2048,768]{1,0:T(8,128)}, f32[2048,768]{1,0:T(8,128)S(1)}, u32[]{:S(2)}) copy-start(f32[2048,768]{1,0:T(8,128)S(1)} %fusion.21) | copy-start | bytes 18874372
  151.7 36.4 %collective-permute-start = (bf16[1024,768]{1,0:T(8,128)(2,1)}, bf16[1024,768]{1,0:T(8,128)(2,1)}, u32[]{:S(2)}, u32[]{:S(2)}) collective-permute-start(bf16[1024,768]{1,0:T(8,128)(2,1)} %dynamic-slice_convert_fusion), channel_id=1, source_target_pairs={{0,16},{16,0},{1,17},{17,1},{2,18},{18,2},{3,19},{19,3},{4,20},{20... | collective-permute-start | bytes 4718600 | tf_op jit(solution)/shard_map/ppermute | solution.py:37
  163.2 1.6 copy-start.3
  164.8 23.6 %copy-start.1 = (f32[1,1024,768]{2,1,0:T(8,128)S(1)}, f32[1,1024,768]{2,1,0:T(8,128)}, u32[]{:S(2)}) copy-start(f32[1,1024,768]{2,1,0:T(8,128)} %param.16) | copy-start | bytes 9437188
  165.8 39.2 %collective-permute-start.2 = (bf16[384,1024]{1,0:T(8,128)(2,1)}, bf16[384,1024]{1,0:T(8,128)(2,1)}, u32[]{:S(2)}, u32[]{:S(2)}) collective-permute-start(bf16[384,1024]{1,0:T(8,128)(2,1)} %dynamic-slice_convert_fusion.1), channel_id=1, source_target_pairs={{0,16},{16,0},{1,17},{17,1},{2,18},{18,2},{3,19},{19,3},{4,20},{20... | collective-permute-start | bytes 2359304 | tf_op jit(solution)/shard_map/ppermute | solution.py:37
  188.4 16.8 %copy-start.4 = (f32[384,2048]{1,0:T(8,128)S(1)}, f32[384,2048]{1,0:T(8,128)}, u32[]{:S(2)}) copy-start(f32[384,2048]{1,0:T(8,128)} %copy-done.3) | copy-start | bytes 9437188
  188.4 16.8 %copy-start.6 = (f32[1,384,1024]{2,1,0:T(8,128)S(1)}, f32[1,384,1024]{2,1,0:T(8,128)}, u32[]{:S(2)}) copy-start(f32[1,384,1024]{2,1,0:T(8,128)} %param.18) | copy-start | bytes 4718596
  188.4 16.8 %copy-start.7 = (f32[1,384,1024]{2,1,0:T(8,128)S(1)}, f32[1,384,1024]{2,1,0:T(8,128)}, u32[]{:S(2)}) copy-start(f32[1,384,1024]{2,1,0:T(8,128)} %param.19) | copy-start | bytes 4718596
  188.4 16.8 %copy-start.10 = (bf16[1,384,2048]{2,1,0:T(8,128)(2,1)S(1)}, bf16[1,384,2048]{2,1,0:T(8,128)(2,1)}, u32[]{:S(2)}) copy-start(bf16[1,384,2048]{2,1,0:T(8,128)(2,1)} %param.15) | copy-start | bytes 4718596
  195.3 13.8 %copy-start.2 = (bf16[1,2048,768]{2,1,0:T(8,128)(2,1)}, bf16[1,2048,768]{2,1,0:T(8,128)(2,1)S(1)}, u32[]{:S(2)}) copy-start(bf16[1,2048,768]{2,1,0:T(8,128)(2,1)S(1)} %get-tuple-element.19) | copy-start | bytes 9437188
  195.3 61.4 %collective-permute-start.1 = (bf16[1,1024,768]{2,1,0:T(8,128)(2,1)}, bf16[1,1024,768]{2,1,0:T(8,128)(2,1)S(1)}, u32[]{:S(2)}, u32[]{:S(2)}) collective-permute-start(bf16[1,1024,768]{2,1,0:T(8,128)(2,1)} %get-tuple-element.20), channel_id=1, source_target_pairs={{0,16},{16,0},{1,17},{17,1},{2,18},{18,2},{3,19},{19,3},{4,20},{20... | collective-permute-start | bytes 4718600 | tf_op jit(solution)/shard_map/ppermute | solution.py:49
  209.2 46.4 %collective-permute-start.3 = (bf16[1,384,1024]{2,1,0:T(8,128)(2,1)}, bf16[1,384,1024]{2,1,0:T(8,128)(2,1)}, u32[]{:S(2)}, u32[]{:S(2)}) collective-permute-start(bf16[1,384,1024]{2,1,0:T(8,128)(2,1)} %get-tuple-element.16), channel_id=1, source_target_pairs={{0,16},{16,0},{1,17},{17,1},{2,18},{18,2},{3,19},{19,3},{4,20},{20... | collective-permute-start | bytes 2359304 | tf_op jit(solution)/shard_map/ppermute | solution.py:49
  256.8 1.7 copy-start.5
Sparse Core Ops, SparseCore 0:
  138.3 105.2 reduce-scatter.1
